TPU v7x, 256 devices: a whole 4x4x8 slice. The times are simulated.
256 devices in a mesh: dp: 4 (over z_lo), ctx: 64 (over z_hi, y, x, core).
Axes of the slice: x: 4, y: 4, z: 8 (z_hi: 2, z_lo: 4; z = z_hi * 4 + z_lo), core: 2. Of those that a mesh axis runs over, the one named last changes fastest.
Arguments:
- qkv: bfloat16 [4, 8192, 6144], P('dp', 'ctx'), may hold values from -6 to 6
- short_filter: float32 [7, 768], replicated, may hold values from -2 to 2
- long_filter: float32 [2048, 8192], P('ctx'), may hold values from -1.1 to 1.1
- cotangent: bfloat16 [4, 8192, 2048], P('dp', 'ctx'), may hold values from -6 to 6
Outputs:
- mixer_out: bfloat16 [4, 8192, 2048], P('dp', 'ctx')
- grad_qkv: bfloat16 [4, 8192, 6144], P('dp', 'ctx')
- grad_long: float32 [2048, 8192], P('ctx')
- grad_short: float32 [7, 768], replicated
All inputs are finite; a program needn't handle non-finite values.
Results may differ from a plain program's by a relative error of at most 0.014.
Values may be sent and summed in bfloat16 or wider, within the bound.
No kernel may reach another device: no remote copies, remote signals or barrier semaphores. Data moves between devices by JAX's collectives and lax.ppermute only.
A program may use at most 128 MiB of HBM per device.

v0:
```python
import math
import jax
import jax.numpy as jnp
from jax import lax
from jax.sharding import PartitionSpec as P

precise = lax.Precision.HIGHEST


def from_behind(array, axis, by):
    devices = lax.axis_size(axis)
    pairs = [(i, i + by) for i in range(devices) if 0 <= i + by < devices]
    return lax.ppermute(array, axis, pairs)


def angles(row_count, col_count, period):
    row_iota = lax.broadcasted_iota(jnp.int32, (row_count, col_count), 0)
    col_iota = lax.broadcasted_iota(jnp.int32, (row_count, col_count), 1)
    return (row_iota * col_iota % period).astype(jnp.float32) * (2.0 * math.pi / period)


def matmul(left_side, right_side):
    return jnp.dot(left_side, right_side, precision=precise, preferred_element_type=jnp.float32)


def column_table(col_count, sign_flip):
    angle_cols = angles(col_count, col_count, col_count)
    cos_part = jnp.cos(angle_cols)
    sin_part = sign_flip * jnp.sin(angle_cols)
    upper = jnp.concatenate([cos_part, sin_part], axis=1)
    lower = jnp.concatenate([-sin_part, cos_part], axis=1)
    return jnp.concatenate([upper, lower], axis=0)


def forward_transform(signal):
    half_rows, own_chans, col_count = signal.shape
    row_count = 2 * half_rows
    total_len = row_count * col_count
    angle_rows = angles(row_count, half_rows, row_count)
    row_table = jnp.concatenate([jnp.cos(angle_rows), -jnp.sin(angle_rows)], axis=0)
    rows_out = matmul(
        row_table, signal.reshape(half_rows, own_chans * col_count).astype(jnp.float32)
    )
    rows_out = rows_out.reshape(2, row_count, own_chans, col_count)
    part_real = rows_out[0]
    part_imag = rows_out[1]
    twist = angles(row_count, col_count, total_len)[:, None, :]
    twist_real = jnp.cos(twist)
    twist_imag = -jnp.sin(twist)
    turned = jnp.concatenate(
        [
            part_real * twist_real - part_imag * twist_imag,
            part_real * twist_imag + part_imag * twist_real,
        ],
        axis=2,
    )
    spec = matmul(
        turned.reshape(row_count * own_chans, 2 * col_count), column_table(col_count, -1.0)
    )
    return spec.reshape(row_count, own_chans, 2 * col_count)


def inverse_transform(spec):
    row_count, own_chans, double_cols = spec.shape
    col_count = double_cols // 2
    half_rows = row_count // 2
    total_len = row_count * col_count
    back = matmul(spec.reshape(row_count * own_chans, double_cols), column_table(col_count, 1.0))
    back = back.reshape(row_count, own_chans, double_cols)
    back_real = back[:, :, :col_count]
    back_imag = back[:, :, col_count:]
    twist = angles(row_count, col_count, total_len)[:, None, :]
    twist_real = jnp.cos(twist)
    twist_imag = jnp.sin(twist)
    turned = jnp.concatenate(
        [
            back_real * twist_real - back_imag * twist_imag,
            back_real * twist_imag + back_imag * twist_real,
        ],
        axis=0,
    )
    angle_rows = angles(half_rows, row_count, row_count)
    row_table = jnp.concatenate([jnp.cos(angle_rows), -jnp.sin(angle_rows)], axis=1) * (
        1.0 / total_len
    )
    result = matmul(row_table, turned.reshape(2 * row_count, own_chans * col_count))
    return result.reshape(half_rows, own_chans, col_count)


def spec_times(first_spec, second_spec, conjugate):
    col_count = first_spec.shape[2] // 2
    first_real = first_spec[:, :, :col_count]
    first_imag = first_spec[:, :, col_count:]
    second_real = second_spec[:, :, :col_count]
    second_imag = conjugate * second_spec[:, :, col_count:]
    return jnp.concatenate(
        [
            first_real * second_real - first_imag * second_imag,
            first_real * second_imag + first_imag * second_real,
        ],
        axis=2,
    )


def shards(qkv, short_filter, long_filter, cotangent):
    seq_rows = qkv[0]
    row_count, width_all = seq_rows.shape
    width = width_all // 3
    tap_count = short_filter.shape[0]
    group_size = width_all // short_filter.shape[1]
    ctx_count = lax.axis_size("ctx")
    own_chans = width // ctx_count
    grad_scale = 1.0 / math.sqrt(lax.axis_size("dp") * ctx_count * row_count)
    tap_weights = jnp.repeat(short_filter, group_size, axis=1)
    left_rim = from_behind(seq_rows[row_count - tap_count + 1 :], "ctx", 1)
    padded = jnp.concatenate([left_rim, seq_rows], axis=0).astype(jnp.float32)
    short_out = jnp.zeros((row_count, width_all), jnp.float32)
    for lag_index in range(tap_count):
        start = tap_count - 1 - lag_index
        short_out = short_out + tap_weights[lag_index] * padded[start : start + row_count]
    query_rows = short_out[:, :width]
    key_rows = short_out[:, width : 2 * width]
    value_rows = short_out[:, 2 * width :]
    cot_rows = cotangent[0].astype(jnp.float32)
    product = (key_rows * value_rows).T.astype(jnp.bfloat16)[None]
    grad_out = (cot_rows * query_rows).T.astype(jnp.bfloat16)[None]
    filter_taps = long_filter.reshape(own_chans, ctx_count, row_count).transpose(1, 0, 2)
    filter_spec = forward_transform(filter_taps)
    own_prod = lax.all_to_all(product, "ctx", split_axis=1, concat_axis=0, tiled=True)
    prod_spec = forward_transform(own_prod)
    y_own = inverse_transform(spec_times(prod_spec, filter_spec, 1.0))
    y_own, prod_spec = (y_own.astype(jnp.bfloat16), prod_spec)
    long_back = lax.all_to_all(y_own, "ctx", split_axis=0, concat_axis=1, tiled=True)
    own_grad = lax.all_to_all(grad_out, "ctx", split_axis=1, concat_axis=0, tiled=True)
    grad_spec = forward_transform(own_grad)
    du_own = inverse_transform(spec_times(grad_spec, filter_spec, -1.0))
    dh_own = inverse_transform(spec_times(grad_spec, prod_spec, -1.0))
    du_own, dh_own = (du_own.astype(jnp.bfloat16), dh_own)
    du_back = lax.all_to_all(du_own, "ctx", split_axis=0, concat_axis=1, tiled=True)
    long_rows = long_back[0].T.astype(jnp.float32)
    mixer_out = (query_rows * long_rows).astype(jnp.bfloat16)[None]
    grad_prod = du_back[0].T.astype(jnp.float32)
    grad_short_out = jnp.concatenate(
        [cot_rows * long_rows, grad_prod * value_rows, grad_prod * key_rows], axis=1
    )
    right_rim = from_behind(grad_short_out[: tap_count - 1].astype(jnp.bfloat16), "ctx", -1).astype(
        jnp.float32
    )
    grad_padded = jnp.concatenate([grad_short_out, right_rim], axis=0)
    grad_rows = jnp.zeros((row_count, width_all), jnp.float32)
    for lag_index in range(tap_count):
        grad_rows = (
            grad_rows + tap_weights[lag_index] * grad_padded[lag_index : lag_index + row_count]
        )
    grad_qkv = grad_rows.astype(jnp.bfloat16)[None]
    lag_terms = []
    for lag_index in range(tap_count):
        start = tap_count - 1 - lag_index
        lag_terms.append(jnp.sum(grad_short_out * padded[start : start + row_count], axis=0))
    short_terms = jnp.stack(lag_terms).reshape(tap_count, -1, group_size).sum(axis=2) * grad_scale
    long_terms = dh_own.transpose(1, 0, 2).reshape(own_chans, ctx_count * row_count) * grad_scale
    grad_short = lax.psum(short_terms, ("dp", "ctx"))
    grad_long = lax.psum(long_terms.astype(jnp.bfloat16), "dp").astype(jnp.float32)
    return (mixer_out, grad_qkv, grad_long, grad_short)


def solution(mesh):
    return jax.shard_map(
        shards,
        mesh=mesh,
        in_specs=(P("dp", "ctx", None), P(), P("ctx", None), P("dp", "ctx", None)),
        out_specs=(P("dp", "ctx", None), P("dp", "ctx", None), P("ctx", None), P()),
        check_vma=False,
    )
```

profile of v0, /device:TPU:1, one launch (start us, length us, event | category | flops | bytes accessed | tf_op | source)
XLA Modules:
  0.0 534.2 jit_solution(974061488572454364)
XLA Ops:
  8.2 4.5 collective-permute-start
  13.0 1.9 copy.39
  15.1 5.7 %fusion.53 = f32[256,4096]{1,0:T(8,128)} fusion(f32[8,8,32,128]{3,2,1,0:T(8,128)S(1)} %bitcast.145, f32[128,64]{1,0:T(8,128)S(1)} %get-tuple-element.64, f32[128,64]{1,0:T(8,128)S(1)} %get-tuple-element.65), kind=kOutput, calls=%fused_computation.90 | convolution fusion | flops 805322752 | bytes 5308416 | tf_op jit(solution)/shard_map/dot_general | solution.py:23
  23.8 1.6 copy.40
  25.4 2.5 maximum_convert_fusion
  28.0 11.8 %multiply_add_fusion = f32[128,6144]{0,1:T(8,128)S(1)} fusion(f32[134,6144]{0,1:T(8,128)S(1)} %maximum_convert_fusion, f32[6144]{0:T(1024)S(1)} %broadcast_in_dim.60, f32[6144]{0:T(1024)S(1)} %broadcast_in_dim.58, f32[6144]{0:T(1024)S(1)} %broadcast_in_dim.56, f32[6144]{0:T(1024)S(1)} %broadcast_in_dim.54, f32[6144]{0:T(1024)S(1)} %broadcast_in_dim.52, ...), kind=kLoop, calls=%fused_computation.57 | loop fusion | flops 10223616 | bytes 25337856 | tf_op jit(solution)/shard_map/add | solution.py:120
  40.0 1.5 copy-done.8
  41.6 8.1 %copy.95 = bf16[1,2048,128]{2,0,1:T(2,128)(2,1)S(1)} copy(bf16[1,2048,128]{2,1,0:T(8,128)(2,1)S(1)} %fusion.62) | data formatting | bytes 1048576 | tf_op jit(solution)/shard_map/broadcast_in_dim | solution.py:126
  50.2 12.0 %reduce.18 = bf16[2048,128]{1,0:T(8,128)(2,1)S(1)} reduce(bf16[2048,1,128]{2,1,0:T(2,128)(2,1)S(1)} %bitcast.143, bf16[]{:T(256)} %broadcast.244), dimensions={1}, to_apply=%bitcast.134.reduce_sub_computation | reduce | bytes 1048578
  63.1 14.1 %all-to-all-start.2 = ((bf16[64,2,2048]{2,1,0:T(2,128)(2,1)}), bf16[64,2,2048]{2,1,0:T(2,128)(2,1)}, u32[]{:S(2)}, u32[]{:S(2)}) async-start(bf16[64,2,2048]{2,1,0:T(2,128)(2,1)} %reshape.246), calls=%async_computation.2 | async-start | bytes 1048576 | tf_op jit(solution)/shard_map/all_to_all | solution.py:134
  77.3 4.7 fusion.130
  82.0 1.9 copy.47
  83.9 1.8 copy.48
  85.7 1.9 copy.49
  87.6 1.8 copy.50
  94.4 3.6 reshape.247
  98.1 8.8 %bitcast_reduce_fusion.1 = bf16[2048,128]{1,0:T(8,128)(2,1)S(1)} fusion(bf16[2048,1,128]{2,1,0:T(2,128)(2,1)S(1)} %reshape.247), kind=kLoop, calls=%fused_computation.202 | loop fusion | bytes 1048576 | tf_op jit(solution)/shard_map/all_to_all | solution.py:134
  107.1 1.8 fusion.73
  108.9 2.4 fusion.129
  111.2 1.9 copy.57
  113.1 1.8 copy.58
  115.0 1.9 copy.59
  116.9 2.0 copy.60
  118.9 4.7 multiply_subtract_fusion.4
  123.6 3.6 fusion.12
  127.3 3.6 fusion.4
  131.6 1.4 copy-done.5
  133.0 3.9 fusion.16
  137.5 2.4 pad_maximum_fusion.2
  139.9 5.6 %copy.63 = f32[256,32,128]{0,2,1:T(8,128)} copy(f32[256,32,128]{2,0,1:T(8,128)} %pad_maximum_fusion.2) | data formatting | bytes 8388608 | tf_op jit(solution)/shard_map/concatenate | solution.py:75
  145.5 6.4 %fusion.49 = bf16[64,32,128]{2,0,1:T(8,128)(2,1)S(1)} fusion(f32[256,32,128]{0,2,1:T(8,128)} %copy.63, f32[64,128]{1,0:T(8,128)S(1)} %copy-done.20, f32[64,128]{1,0:T(8,128)S(1)} %copy-done.22), kind=kOutput, calls=%fused_computation.88 | convolution fusion | flops 805601280 | bytes 4784128 | tf_op jit(solution)/shard_map/dot_general | solution.py:23
  152.3 29.5 %all_to_all.16 = bf16[64,32,128]{2,1,0:T(8,128)(2,1)S(1)} all-to-all(bf16[64,32,128]{2,1,0:T(8,128)(2,1)S(1)} %copy.64), channel_id=1, replica_groups=mesh['dp'=4,'ctx'=64] {'ctx'}, dimensions={0} | all-to-all | bytes 1048576 | tf_op jit(solution)/shard_map/all_to_all | solution.py:139
  182.0 8.1 %copy.96 = bf16[1,2048,128]{2,0,1:T(2,128)(2,1)S(1)} copy(bf16[1,2048,128]{2,1,0:T(8,128)(2,1)S(1)} %get-tuple-element.57) | data formatting | bytes 1048576 | tf_op jit(solution)/shard_map/broadcast_in_dim | solution.py:125
  190.2 12.3 %reduce.19 = bf16[2048,128]{1,0:T(8,128)(2,1)} reduce(bf16[2048,1,128]{2,1,0:T(2,128)(2,1)S(1)} %bitcast.144, bf16[]{:T(256)} %broadcast.244), dimensions={1}, to_apply=%bitcast.135.reduce_sub_computation | reduce | bytes 1048578
  203.7 21.0 %all_to_all.17 = bf16[64,2,2048]{2,1,0:T(2,128)(2,1)} all-to-all(bf16[64,2,2048]{2,1,0:T(2,128)(2,1)S(1)} %reshape.248), channel_id=1, replica_groups=mesh['dp'=4,'ctx'=64] {'ctx'}, dimensions={0} | all-to-all | bytes 1048576 | tf_op jit(solution)/shard_map/all_to_all | solution.py:129
  224.7 3.6 reshape.249
  228.3 9.6 %bitcast_reduce_fusion = bf16[2048,128]{1,0:T(8,128)(2,1)} fusion(bf16[2048,1,128]{2,1,0:T(2,128)(2,1)S(1)} %reshape.249), kind=kLoop, calls=%fused_computation.201 | loop fusion | bytes 1048576 | tf_op jit(solution)/shard_map/all_to_all | solution.py:129
  239.1 1.8 fusion.74
  242.6 5.0 fusion
  247.7 6.2 %multiply_subtract_fusion.1 = (f32[128,32,128]{2,0,1:T(8,128)}, f32[128,32,128]{2,0,1:T(8,128)}, f32[128,32,128]{2,0,1:T(8,128)S(1)}, f32[128,32,128]{2,0,1:T(8,128)}) fusion(f32[128,32,256]{2,0,1:T(8,128)S(1)} %copy-done.4, f32[128,32,256]{2,0,1:T(8,128)} %fusion, f32[128,32,256]{2,0,1:T(8,128)S(1)} %copy-done.6), kind=kLoop, calls=%fused_computation.69 | loop fusion | flops 6815744 | bytes 20971520 | tf_op jit(solution)/shard_map/sub | solution.py:98
  253.9 5.7 %fusion.20 = f32[128,32,256]{2,0,1:T(8,128)S(1)} fusion(f32[128,32,128]{2,0,1:T(8,128)} %get-tuple-element.30, f32[128,32,128]{2,0,1:T(8,128)} %get-tuple-element.29, f32[128,128]{1,0:T(8,128)S(1)} %get-tuple-element.69, f32[128,128]{1,0:T(8,128)S(1)} %get-tuple-element.71, f32[128,128]{1,0:T(8,128)S(1)} %get-tuple-element.70), kind=kOutput, calls=%fused_computation.23 | convolution fusion | flops 3222470656 | bytes 8585216 | tf_op jit(solution)/shard_map/dot_general | solution.py:23
  259.6 3.6 fusion.8
  263.2 2.9 multiply_subtract_fusion
  266.1 2.4 pad_maximum_fusion.1
  268.5 5.6 %copy.53 = f32[256,32,128]{0,2,1:T(8,128)} copy(f32[256,32,128]{2,0,1:T(8,128)} %pad_maximum_fusion.1) | data formatting | bytes 8388608 | tf_op jit(solution)/shard_map/concatenate | solution.py:75
  274.1 6.2 %fusion.46 = bf16[64,32,128]{2,0,1:T(8,128)(2,1)S(1)} fusion(f32[256,32,128]{0,2,1:T(8,128)} %copy.53, f32[64,128]{1,0:T(8,128)S(1)} %copy-done.21, f32[64,128]{1,0:T(8,128)S(1)} %copy-done.23), kind=kOutput, calls=%fused_computation.87 | convolution fusion | flops 805601280 | bytes 4784128 | tf_op jit(solution)/shard_map/dot_general | solution.py:23
  281.4 9.5 %all-to-all-start.1 = ((bf16[64,32,128]{2,1,0:T(8,128)(2,1)}), bf16[64,32,128]{2,1,0:T(8,128)(2,1)}, u32[]{:S(2)}, u32[]{:S(2)}) async-start(bf16[64,32,128]{2,1,0:T(8,128)(2,1)} %copy.54), calls=%async_computation.1 | async-start | bytes 1048576 | tf_op jit(solution)/shard_map/all_to_all | solution.py:133
  291.0 4.7 pad_maximum_fusion.3
  295.7 6.0 %copy.67 = f32[256,32,128]{0,2,1:T(8,128)} copy(f32[256,32,128]{2,0,1:T(8,128)} %pad_maximum_fusion.3) | data formatting | bytes 8388608 | tf_op jit(solution)/shard_map/concatenate | solution.py:75
  301.7 6.2 %fusion.43 = bf16[64,32,128]{2,0,1:T(8,128)(2,1)S(1)} fusion(f32[256,32,128]{0,2,1:T(8,128)} %copy.67, f32[64,128]{1,0:T(8,128)S(1)} %copy-done.21, f32[64,128]{1,0:T(8,128)S(1)} %copy-done.23), kind=kOutput, calls=%fused_computation.86 | convolution fusion | flops 805863424 | bytes 4784128 | tf_op jit(solution)/shard_map/dot_general | solution.py:23
  309.0 55.1 %all-reduce.2.cloned.1.call-done = bf16[32,8192]{1,0:T(8,128)(2,1)} async-done(((bf16[32,8192]{1,0:T(8,128)(2,1)}), bf16[32,8192]{1,0:T(8,128)(2,1)}) %all-reduce.2.cloned.1.call-update) | async-done | bytes 524304 | tf_op jit(solution)/shard_map/psum | solution.py:163
  364.1 2.1 convert_element_type.194
  366.2 2.5 convert_multiply_fusion.1
  368.7 27.9 %multiply_reduce_fusion = (f32[6144]{0:T(1024)}, f32[6144]{0:T(1024)}, f32[6144]{0:T(1024)}, f32[6144]{0:T(1024)}, f32[6144]{0:T(1024)}, /*index=5*/f32[6144]{0:T(1024)}, f32[6144]{0:T(1024)}) fusion(f32[134,6144]{0,1:T(8,128)} %copy-done.2, f32[128,2048]{0,1:T(8,128)S(1)} %get-tuple-element.56, f32[128,2048]{0,1:T(8,128)S(1)} %get-tuple-element.55, ...), kind=kLoop, calls=%fused_computation.50 | loop fusion | flops 12539904 | bytes 25337856 | tf_op jit(solution)/shard_map/reduce_sum | solution.py:159
  411.3 1.7 copy.65
  413.0 4.6 collective-permute-start.1
  417.6 1.4 constant_dynamic-update-slice_fusion.5
  419.0 1.3 constant_dynamic-update-slice_fusion.4
  426.7 2.0 copy.75
  428.7 77.5 %psum.15 = f32[7,768]{1,0:T(8,128)} all-reduce(f32[7,768]{1,0:T(8,128)S(1)} %broadcast_multiply_fusion.1), channel_id=1, replica_groups=mesh['dp'=4,'ctx'=64] {'dp','ctx'}, use_global_device_ids=true, to_apply=%region_9.10 | all-reduce | flops 5376 | bytes 43008 | tf_op jit(solution)/shard_map/psum | solution.py:162
  506.3 2.0 copy.66
  508.3 2.4 pad_maximum_fusion
  510.8 13.7 %fusion.39 = bf16[1,128,6144]{1,2,0:T(8,128)(2,1)} fusion(f32[134,6144]{0,1:T(8,128)S(1)} %pad_maximum_fusion, f32[6144]{0:T(1024)S(1)} %copy-done.36, f32[6144]{0:T(1024)S(1)} %copy-done.38, f32[6144]{0:T(1024)S(1)} %copy-done.28, f32[6144]{0:T(1024)S(1)} %copy-done.30, f32[6144]{0:T(1024)S(1)} %copy-done.32, f32[6144]{0:T(1024)S(1)} %copy-done.34, ...), kind=kLoop, calls=%fused_computation.82 | loop fusion | flops 12582912 | bytes 23764992 | tf_op jit(solution)/shard_map/broadcast_in_dim | solution.py:155
  524.6 2.6 copy.76
  (145 shorter events, 40.5 us)
Async XLA Ops:
  7.2 7.7 %copy-start = (f32[32,8192]{1,0:T(8,128)S(1)}, f32[32,8192]{1,0:T(8,128)}, u32[]{:S(2)}) copy-start(f32[32,8192]{1,0:T(8,128)} %param.6) | copy-start | bytes 3145732
  8.2 15.6 %collective-permute-start = (bf16[6,6144]{1,0:T(8,128)(2,1)S(1)}, bf16[6,6144]{1,0:T(8,128)(2,1)S(1)}, u32[]{:S(2)}, u32[]{:S(2)}) collective-permute-start(bf16[6,6144]{1,0:T(8,128)(2,1)S(1)} %slice_bitcast_fusion.2), channel_id=1, source_target_pairs={{0,1},{1,2},{2,3},{3,4},{4,5},{5,6},{6,7},{7,8},{8,9},{9,10},{10,1... | collective-permute-start | bytes 221192 | tf_op jit(solution)/shard_map/ppermute | solution.py:13
  15.1 5.7 %copy-start.39 = (f32[7,768]{1,0:T(8,128)S(1)}, f32[7,768]{1,0:T(8,128)}, u32[]{:S(2)}) copy-start(f32[7,768]{1,0:T(8,128)} %param.5) | copy-start | bytes 64516
  20.8 2.7 copy-start.24
  21.2 6.8 %copy-start.25 = (f32[6144]{0:T(1024)}, f32[6144]{0:T(1024)S(1)}, u32[]{:S(2)}) copy-start(f32[6144]{0:T(1024)S(1)} %broadcast_in_dim.48) | copy-start | bytes 73732
  21.6 6.4 %copy-start.27 = (f32[6144]{0:T(1024)}, f32[6144]{0:T(1024)S(1)}, u32[]{:S(2)}) copy-start(f32[6144]{0:T(1024)S(1)} %broadcast_in_dim.56) | copy-start | bytes 73732
  22.0 6.0 %copy-start.29 = (f32[6144]{0:T(1024)}, f32[6144]{0:T(1024)S(1)}, u32[]{:S(2)}) copy-start(f32[6144]{0:T(1024)S(1)} %broadcast_in_dim.54) | copy-start | bytes 73732
  22.4 5.6 %copy-start.31 = (f32[6144]{0:T(1024)}, f32[6144]{0:T(1024)S(1)}, u32[]{:S(2)}) copy-start(f32[6144]{0:T(1024)S(1)} %broadcast_in_dim.52) | copy-start | bytes 73732
  22.7 5.3 copy-start.33
  23.1 4.9 copy-start.35
  23.5 4.5 copy-start.37
  23.8 16.1 %copy-start.11 = (bf16[1,128,2048]{1,2,0:T(8,128)(2,1)}, bf16[1,128,2048]{1,2,0:T(8,128)(2,1)S(1)}, u32[]{:S(2)}) copy-start(bf16[1,128,2048]{1,2,0:T(8,128)(2,1)S(1)} %copy.55) | copy-start | bytes 1572868
  28.0 11.9 %copy-start.2 = (f32[134,6144]{0,1:T(8,128)}, f32[134,6144]{0,1:T(8,128)S(1)}, u32[]{:S(2)}) copy-start(f32[134,6144]{0,1:T(8,128)S(1)} %maximum_convert_fusion) | copy-start | bytes 9879556
  39.9 1.7 copy-start.8
  63.1 31.3 %all-to-all-start.2 = ((bf16[64,2,2048]{2,1,0:T(2,128)(2,1)}), bf16[64,2,2048]{2,1,0:T(2,128)(2,1)}, u32[]{:S(2)}, u32[]{:S(2)}) async-start(bf16[64,2,2048]{2,1,0:T(2,128)(2,1)} %reshape.246), calls=%async_computation.2 | async-start | bytes 1048576 | tf_op jit(solution)/shard_map/all_to_all | solution.py:134
  116.9 2.0 copy-start.18
  118.9 4.7 copy-start.12
  118.9 4.7 copy-start.14
  127.3 3.6 copy-start.3
  130.9 2.1 copy-start.5
  133.0 3.9 copy-start.16
  139.9 5.6 %copy-start.20 = (f32[64,128]{1,0:T(8,128)S(1)}, f32[64,128]{1,0:T(8,128)}, u32[]{:S(2)}) copy-start(f32[64,128]{1,0:T(8,128)} %get-tuple-element.72) | copy-start | bytes 98308
  139.9 5.6 %copy-start.22 = (f32[64,128]{1,0:T(8,128)S(1)}, f32[64,128]{1,0:T(8,128)}, u32[]{:S(2)}) copy-start(f32[64,128]{1,0:T(8,128)} %get-tuple-element.73) | copy-start | bytes 98308
  145.5 36.3 %copy-start.9 = (f32[128,6144]{0,1:T(8,128)S(1)}, f32[128,6144]{0,1:T(8,128)}, u32[]{:S(2)}) copy-start(f32[128,6144]{0,1:T(8,128)} %copy-done.8) | copy-start | bytes 9437188
  240.9 0.8 copy-start.19
  241.8 0.8 copy-start.13
  241.8 0.9 copy-start.15
  242.6 5.0 copy-start.4
  242.6 5.0 copy-start.6
  253.9 5.7 %copy-start.10 = (f32[128,32,128]{2,0,1:T(8,128)S(1)}, f32[128,32,128]{2,0,1:T(8,128)}, u32[]{:S(2)}) copy-start(f32[128,32,128]{2,0,1:T(8,128)} %get-tuple-element.48) | copy-start | bytes 6291460
  259.6 3.6 copy-start.17
  268.5 5.6 %copy-start.21 = (f32[64,128]{1,0:T(8,128)S(1)}, f32[64,128]{1,0:T(8,128)}, u32[]{:S(2)}) copy-start(f32[64,128]{1,0:T(8,128)} %get-tuple-element.72) | copy-start | bytes 98308
  268.5 5.6 %copy-start.23 = (f32[64,128]{1,0:T(8,128)S(1)}, f32[64,128]{1,0:T(8,128)}, u32[]{:S(2)}) copy-start(f32[64,128]{1,0:T(8,128)} %get-tuple-element.73) | copy-start | bytes 98308
  281.4 84.8 %all-to-all-start.1 = ((bf16[64,32,128]{2,1,0:T(8,128)(2,1)}), bf16[64,32,128]{2,1,0:T(8,128)(2,1)}, u32[]{:S(2)}, u32[]{:S(2)}) async-start(bf16[64,32,128]{2,1,0:T(8,128)(2,1)} %copy.54), calls=%async_computation.1 | async-start | bytes 1048576 | tf_op jit(solution)/shard_map/all_to_all | solution.py:133
  290.9 73.2 %all-reduce.2.cloned.1.call-start = ((), (), s32[]{:S(2)}) async-start(), calls=%async_computation.4 | async-start | bytes 1048576 | tf_op jit(solution)/shard_map/psum | solution.py:163
  368.7 139.6 %copy-start.7 = (f32[128,2048]{0,1:T(8,128)}, f32[128,2048]{0,1:T(8,128)S(1)}, u32[]{:S(2)}) copy-start(f32[128,2048]{0,1:T(8,128)S(1)} %get-tuple-element.58) | copy-start | bytes 3145732
  413.0 93.2 %collective-permute-start.1 = (bf16[6,6144]{1,0:T(8,128)(2,1)S(1)}, bf16[6,6144]{1,0:T(8,128)(2,1)S(1)}, u32[]{:S(2)}, u32[]{:S(2)}) collective-permute-start(bf16[6,6144]{1,0:T(8,128)(2,1)S(1)} %copy.65), channel_id=1, source_target_pairs={{1,0},{2,1},{3,2},{4,3},{5,4},{6,5},{7,6},{8,7},{9,8},{10,9},{11,1... | collective-permute-start | bytes 221192 | tf_op jit(solution)/shard_map/ppermute | solution.py:13
  508.3 2.5 copy-start.26
  508.3 2.5 copy-start.28
  508.3 2.5 copy-start.30
  508.3 2.5 copy-start.32
  508.3 2.5 copy-start.34
  508.3 2.5 copy-start.36
  508.3 2.5 copy-start.38
  510.8 16.3 %copy-start.1 = (f32[32,8192]{1,0:T(8,128)S(1)}, f32[32,8192]{1,0:T(8,128)}, u32[]{:S(2)}) copy-start(f32[32,8192]{1,0:T(8,128)} %param.6) | copy-start | bytes 3145732
Sparse Core Ops, SparseCore 0:
  309.2 54.9 all-reduce.1
where the time goes:
time: 545 us; the launch traced here: 534 us
  local copies, waits for them, and re-layouts  129 us (24%)
  blocking collectives  128 us (23%)
  other arithmetic  120 us (22%)
  waiting for transfers between devices  55.4 us (10%)
  matrix products  53.4 us (10%)
  starting transfers between devices  32.8 us (6%)
  between operations  15.1 us (3%)
    psum x1, blocking collectives, shards(): grad_short = lax.psum(short_terms, ('dp', 'ctx'))  77.5 us
    psum x1, waiting for transfers between devices, shards(): lax.psum(long_terms.astype(jnp.bfloat16), 'dp').astype(jnp.float32)  55.1 us
    dot_general x12, matrix products, matmul(): jnp.dot(left_side, right_side, precision=precise, preferred_element_type=...  53.4 us
    unnamed x97, local copies, waits for them, and re-layouts  30 us
    all_to_all x1, blocking collectives, shards(): lax.all_to_all(du_own, 'ctx', split_axis=0, concat_axis=1, tiled=True)  29.5 us
    reduce_sum x1, other arithmetic, shards(): jnp.sum(grad_short_out * padded[start:start + row_count], axis=0)  27.9 us
    unnamed x2, other arithmetic  24.3 us
    all_to_all x1, blocking collectives, shards(): lax.all_to_all(product, 'ctx', split_axis=1, concat_axis=0, tiled=True)  21 us
  transfers between devices with their start and end apart: 5, of which 2 were waited for; matrix products, arithmetic and copies ran while one was open for 11% of the time, Pallas kernels for 0%

commit v1 on v0

--- a/solution.py
+++ b/solution.py
@@ -159,7 +159,7 @@
         lag_terms.append(jnp.sum(grad_short_out * padded[start : start + row_count], axis=0))
     short_terms = jnp.stack(lag_terms).reshape(tap_count, -1, group_size).sum(axis=2) * grad_scale
     long_terms = dh_own.transpose(1, 0, 2).reshape(own_chans, ctx_count * row_count) * grad_scale
-    grad_short = lax.psum(short_terms, ("dp", "ctx"))
+    grad_short = jnp.sum(lax.all_gather(short_terms, ("dp", "ctx")), axis=0)
     grad_long = lax.psum(long_terms.astype(jnp.bfloat16), "dp").astype(jnp.float32)
     return (mixer_out, grad_qkv, grad_long, grad_short)
 

time: 545 us -> 824 us (1.51)
  waiting for transfers between devices: 55.4 us -> 396 us
  blocking collectives: 128 us -> 49.8 us
  other arithmetic: 120 us -> 134 us
    all_gather x0 -> x1, waiting for transfers between devices: none -> 395 us  [shards(): grad_short = jnp.sum(lax.all_gather(short_terms, ('dp', 'ctx')), axis=0)]
    psum x1 -> x0, blocking collectives: 77.5 us -> none  [shards(): grad_short = lax.psum(short_terms, ('dp', 'ctx'))]
    psum x1, waiting for transfers between devices: 55.1 us -> 0.02 us  [shards(): lax.psum(long_terms.astype(jnp.bfloat16), 'dp').astype(jnp.float32)]
    unnamed x2 -> x3, other arithmetic: 24.3 us -> 38.4 us
    unnamed x97 -> x95, local copies, waits for them, and re-layouts: 30 us -> 30.5 us
  transfers between devices with their start and end apart: 5 -> 6, of which waited for: 2 -> 2; matrix products, arithmetic and copies ran while one was open for 11% -> 15% of each run, Pallas kernels for 0% -> 0%
where the time goes in v1:
time: 824 us; the launch traced here: 812 us
  waiting for transfers between devices  396 us (48%)
  other arithmetic  134 us (16%)
  local copies, waits for them, and re-layouts  133 us (16%)
  matrix products  53.1 us (6%)
  blocking collectives  49.8 us (6%)
  starting transfers between devices  30.6 us (4%)
  between operations  16.7 us (2%)
    all_gather x1, waiting for transfers between devices, shards(): grad_short = jnp.sum(lax.all_gather(short_terms, ('dp', 'ctx')), axis=0)  395 us
    dot_general x12, matrix products, matmul(): jnp.dot(left_side, right_side, precision=precise, preferred_element_type=...  53.1 us
    unnamed x3, other arithmetic  38.4 us
    unnamed x95, local copies, waits for them, and re-layouts  30.5 us
    all_to_all x1, blocking collectives, shards(): lax.all_to_all(du_own, 'ctx', split_axis=0, concat_axis=1, tiled=True)  28.6 us
    reduce_sum x1, other arithmetic, shards(): jnp.sum(grad_short_out * padded[start:start + row_count], axis=0)  27.9 us
    all_to_all x1, blocking collectives, shards(): lax.all_to_all(product, 'ctx', split_axis=1, concat_axis=0, tiled=True)  21.2 us
    concatenate x3, local copies, waits for them, and re-layouts, inverse_transform(): jnp.concatenate([back_real * twist_real - back_imag * twist_imag, back_re...  16.8 us
  transfers between devices with their start and end apart: 6, of which 2 were waited for; matrix products, arithmetic and copies ran while one was open for 15% of the time, Pallas kernels for 0%

profile of v1, /device:TPU:1, one launch (start us, length us, event | category | flops | bytes accessed | tf_op | source)
XLA Modules:
  0.0 812.5 jit_solution(14999447456414787757)
XLA Ops:
  9.0 4.5 collective-permute-start
  13.8 1.9 copy.39
  15.9 5.7 fusion.53
  25.3 1.6 copy.40
  26.9 2.5 maximum_convert_fusion
  29.6 11.8 %multiply_add_fusion = f32[128,6144]{0,1:T(8,128)S(1)} fusion(f32[134,6144]{0,1:T(8,128)S(1)} %maximum_convert_fusion, f32[6144]{0:T(1024)S(1)} %broadcast_in_dim.60, f32[6144]{0:T(1024)S(1)} %broadcast_in_dim.58, f32[6144]{0:T(1024)S(1)} %broadcast_in_dim.56, f32[6144]{0:T(1024)S(1)} %broadcast_in_dim.54, f32[6144]{0:T(1024)S(1)} %broadcast_in_dim.52, ...), kind=kLoop, calls=%fused_computation.57 | loop fusion | flops 10223616 | bytes 25337856 | tf_op jit(solution)/shard_map/add | solution.py:120
  41.6 8.9 %copy.95 = bf16[1,2048,128]{2,0,1:T(2,128)(2,1)} copy(bf16[1,2048,128]{2,1,0:T(8,128)(2,1)S(1)} %fusion.62) | data formatting | bytes 1048576 | tf_op jit(solution)/shard_map/broadcast_in_dim | solution.py:126
  51.1 25.4 %reduce.19 = bf16[2048,128]{1,0:T(8,128)(2,1)} reduce(bf16[2048,1,128]{2,1,0:T(2,128)(2,1)} %bitcast.145, bf16[]{:T(256)} %broadcast.253), dimensions={1}, to_apply=%bitcast.136.reduce_sub_computation | reduce | bytes 1048578
  76.5 2.0 reshape.259
  78.4 14.1 %all-to-all-start.2 = ((bf16[64,2,2048]{2,1,0:T(2,128)(2,1)}), bf16[64,2,2048]{2,1,0:T(2,128)(2,1)}, u32[]{:S(2)}, u32[]{:S(2)}) async-start(bf16[64,2,2048]{2,1,0:T(2,128)(2,1)} %reshape.259), calls=%async_computation.2 | async-start | bytes 1048576 | tf_op jit(solution)/shard_map/all_to_all | solution.py:134
  92.6 4.7 fusion.130
  97.3 2.9 copy.47
  100.2 2.9 copy.48
  103.1 1.9 copy.49
  105.0 1.9 copy.50
  109.7 3.6 reshape.260
  113.4 8.8 %bitcast_reduce_fusion.1 = bf16[2048,128]{1,0:T(8,128)(2,1)S(1)} fusion(bf16[2048,1,128]{2,1,0:T(2,128)(2,1)S(1)} %reshape.260), kind=kLoop, calls=%fused_computation.202 | loop fusion | bytes 1048576 | tf_op jit(solution)/shard_map/all_to_all | solution.py:134
  122.4 1.8 fusion.73
  124.1 2.4 fusion.129
  126.5 1.9 copy.57
  128.4 1.8 copy.58
  130.3 1.9 copy.59
  132.2 2.2 copy.60
  134.4 4.6 multiply_subtract_fusion.4
  139.0 3.6 fusion.12
  142.7 3.6 fusion.4
  147.0 1.5 copy-done.5
  148.4 3.6 fusion.16
  152.5 2.4 pad_maximum_fusion.2
  155.0 5.6 copy.63
  160.6 6.4 fusion.49
  167.3 28.6 %all_to_all.16 = bf16[64,32,128]{2,1,0:T(8,128)(2,1)S(1)} all-to-all(bf16[64,32,128]{2,1,0:T(8,128)(2,1)S(1)} %copy.64), channel_id=1, replica_groups=mesh['dp'=4,'ctx'=64] {'ctx'}, dimensions={0} | all-to-all | bytes 1048576 | tf_op jit(solution)/shard_map/all_to_all | solution.py:139
  196.1 8.1 %copy.96 = bf16[1,2048,128]{2,0,1:T(2,128)(2,1)S(1)} copy(bf16[1,2048,128]{2,1,0:T(8,128)(2,1)S(1)} %get-tuple-element.57) | data formatting | bytes 1048576 | tf_op jit(solution)/shard_map/broadcast_in_dim | solution.py:125
  204.3 12.4 %reduce.20 = bf16[2048,128]{1,0:T(8,128)(2,1)} reduce(bf16[2048,1,128]{2,1,0:T(2,128)(2,1)S(1)} %bitcast.146, bf16[]{:T(256)} %broadcast.253), dimensions={1}, to_apply=%bitcast.137.reduce_sub_computation | reduce | bytes 1048578
  217.8 21.2 %all_to_all.17 = bf16[64,2,2048]{2,1,0:T(2,128)(2,1)} all-to-all(bf16[64,2,2048]{2,1,0:T(2,128)(2,1)S(1)} %reshape.261), channel_id=1, replica_groups=mesh['dp'=4,'ctx'=64] {'ctx'}, dimensions={0} | all-to-all | bytes 1048576 | tf_op jit(solution)/shard_map/all_to_all | solution.py:129
  239.1 3.6 reshape.262
  242.7 9.6 %bitcast_reduce_fusion = bf16[2048,128]{1,0:T(8,128)(2,1)} fusion(bf16[2048,1,128]{2,1,0:T(2,128)(2,1)S(1)} %reshape.262), kind=kLoop, calls=%fused_computation.201 | loop fusion | bytes 1048576 | tf_op jit(solution)/shard_map/all_to_all | solution.py:129
  253.5 1.8 fusion.74
  257.0 5.0 fusion
  262.0 6.3 multiply_subtract_fusion.1
  268.3 5.6 fusion.20
  273.9 3.6 fusion.8
  277.5 2.9 multiply_subtract_fusion
  280.4 2.4 pad_maximum_fusion.1
  282.8 5.6 copy.53
  288.4 6.2 fusion.46
  295.7 9.5 %all-to-all-start.1 = ((bf16[64,32,128]{2,1,0:T(8,128)(2,1)}), bf16[64,32,128]{2,1,0:T(8,128)(2,1)}, u32[]{:S(2)}, u32[]{:S(2)}) async-start(bf16[64,32,128]{2,1,0:T(8,128)(2,1)} %copy.54), calls=%async_computation.1 | async-start | bytes 1048576 | tf_op jit(solution)/shard_map/all_to_all | solution.py:133
  305.3 4.7 pad_maximum_fusion.3
  310.0 5.6 copy.67
  315.6 6.2 fusion.43
  323.0 2.5 convert_multiply_fusion.1
  325.5 27.9 %multiply_reduce_fusion = (f32[6144]{0:T(1024)}, f32[6144]{0:T(1024)}, f32[6144]{0:T(1024)}, f32[6144]{0:T(1024)}, f32[6144]{0:T(1024)}, /*index=5*/f32[6144]{0:T(1024)}, f32[6144]{0:T(1024)}) fusion(f32[134,6144]{0,1:T(8,128)} %copy-done.2, f32[128,2048]{0,1:T(8,128)S(1)} %get-tuple-element.56, f32[128,2048]{0,1:T(8,128)S(1)} %get-tuple-element.55, ...), kind=kLoop, calls=%fused_computation.50 | loop fusion | flops 12539904 | bytes 25337856 | tf_op jit(solution)/shard_map/reduce_sum | solution.py:159
  366.8 1.3 constant_dynamic-update-slice_fusion.5
  369.5 1.3 constant_dynamic-update-slice_fusion.3
  377.8 1.7 copy.65
  379.5 2.4 collective-permute-start.1
  382.0 2.1 convert_element_type.194
  384.1 2.0 copy.75
  386.1 2.1 copy.66
  388.3 2.4 pad_maximum_fusion
  390.8 12.6 %fusion.39 = bf16[1,128,6144]{1,2,0:T(8,128)(2,1)} fusion(f32[134,6144]{0,1:T(8,128)S(1)} %pad_maximum_fusion, f32[6144]{0:T(1024)S(1)} %copy-done.35, f32[6144]{0:T(1024)S(1)} %copy-done.37, f32[6144]{0:T(1024)S(1)} %copy-done.27, f32[6144]{0:T(1024)S(1)} %copy-done.29, f32[6144]{0:T(1024)S(1)} %copy-done.31, f32[6144]{0:T(1024)S(1)} %copy-done.33, ...), kind=kLoop, calls=%fused_computation.82 | loop fusion | flops 12582912 | bytes 23764992 | tf_op jit(solution)/shard_map/broadcast_in_dim | solution.py:155
  403.3 2.7 copy.76
  406.0 394.7 %all-gather.4.cloned.1.call-done = f32[256,7,768]{2,1,0:T(8,128)} async-done(((f32[1,7,768]{2,1,0:T(8,128)}), f32[256,7,768]{2,1,0:T(8,128)}) %all-gather.4.cloned.1.call-update) | async-done | bytes 5505040 | tf_op jit(solution)/shard_map/all_gather | solution.py:162
  800.7 3.9 reduce_sum.89
  (146 shorter events, 38.6 us)
Async XLA Ops:
  8.0 7.7 copy-start
  9.0 16.3 %collective-permute-start = (bf16[6,6144]{1,0:T(8,128)(2,1)S(1)}, bf16[6,6144]{1,0:T(8,128)(2,1)S(1)}, u32[]{:S(2)}, u32[]{:S(2)}) collective-permute-start(bf16[6,6144]{1,0:T(8,128)(2,1)S(1)} %slice_bitcast_fusion.2), channel_id=1, source_target_pairs={{0,1},{1,2},{2,3},{3,4},{4,5},{5,6},{6,7},{7,8},{8,9},{9,10},{10,1... | collective-permute-start | bytes 221192 | tf_op jit(solution)/shard_map/ppermute | solution.py:13
  15.9 5.7 copy-start.38
  21.6 2.7 copy-start.23
  22.0 7.4 copy-start.24
  22.4 7.1 copy-start.26
  22.8 6.7 copy-start.28
  23.2 6.3 copy-start.30
  23.5 6.0 copy-start.32
  23.9 5.6 copy-start.34
  24.3 5.2 copy-start.36
  29.5 11.9 %copy-start.2 = (f32[134,6144]{0,1:T(8,128)}, f32[134,6144]{0,1:T(8,128)S(1)}, u32[]{:S(2)}) copy-start(f32[134,6144]{0,1:T(8,128)S(1)} %maximum_convert_fusion) | copy-start | bytes 9879556
  29.5 11.9 %copy-start.10 = (bf16[1,128,2048]{1,2,0:T(8,128)(2,1)S(1)}, bf16[1,128,2048]{1,2,0:T(8,128)(2,1)}, u32[]{:S(2)}) copy-start(bf16[1,128,2048]{1,2,0:T(8,128)(2,1)} %copy.55) | copy-start | bytes 1572868
  41.4 58.8 %copy-start.7 = (f32[128,6144]{0,1:T(8,128)}, f32[128,6144]{0,1:T(8,128)S(1)}, u32[]{:S(2)}) copy-start(f32[128,6144]{0,1:T(8,128)S(1)} %multiply_add_fusion) | copy-start | bytes 9437188
  78.4 31.3 %all-to-all-start.2 = ((bf16[64,2,2048]{2,1,0:T(2,128)(2,1)}), bf16[64,2,2048]{2,1,0:T(2,128)(2,1)}, u32[]{:S(2)}, u32[]{:S(2)}) async-start(bf16[64,2,2048]{2,1,0:T(2,128)(2,1)} %reshape.259), calls=%async_computation.2 | async-start | bytes 1048576 | tf_op jit(solution)/shard_map/all_to_all | solution.py:134
  107.1 35.6 %copy-start.11 = (f32[128,128]{1,0:T(8,128)}, f32[128,128]{1,0:T(8,128)S(1)}, u32[]{:S(2)}) copy-start(f32[128,128]{1,0:T(8,128)S(1)} %fusion.112) | copy-start | bytes 196612
  107.4 44.6 %copy-start.15 = (f32[128,128]{1,0:T(8,128)}, f32[128,128]{1,0:T(8,128)S(1)}, u32[]{:S(2)}) copy-start(f32[128,128]{1,0:T(8,128)S(1)} %fusion.101) | copy-start | bytes 196612
  107.6 53.0 %copy-start.19 = (f32[64,128]{1,0:T(8,128)}, f32[64,128]{1,0:T(8,128)S(1)}, u32[]{:S(2)}) copy-start(f32[64,128]{1,0:T(8,128)S(1)} %get-tuple-element.72) | copy-start | bytes 98308
  107.6 53.0 %copy-start.21 = (f32[64,128]{1,0:T(8,128)}, f32[64,128]{1,0:T(8,128)S(1)}, u32[]{:S(2)}) copy-start(f32[64,128]{1,0:T(8,128)S(1)} %get-tuple-element.73) | copy-start | bytes 98308
  107.9 26.5 %copy-start.17 = (f32[128,128]{1,0:T(8,128)}, f32[128,128]{1,0:T(8,128)S(1)}, u32[]{:S(2)}) copy-start(f32[128,128]{1,0:T(8,128)S(1)} %get-tuple-element.67) | copy-start | bytes 196612
  108.4 34.3 %copy-start.13 = (f32[128,128]{1,0:T(8,128)}, f32[128,128]{1,0:T(8,128)S(1)}, u32[]{:S(2)}) copy-start(f32[128,128]{1,0:T(8,128)S(1)} %get-tuple-element.68) | copy-start | bytes 196612
  142.7 3.7 copy-start.3
  146.3 2.1 copy-start.5
  160.6 35.3 %copy-start.8 = (f32[128,6144]{0,1:T(8,128)S(1)}, f32[128,6144]{0,1:T(8,128)}, u32[]{:S(2)}) copy-start(f32[128,6144]{0,1:T(8,128)} %copy-done.7) | copy-start | bytes 9437188
  255.3 0.8 copy-start.18
  256.1 0.8 copy-start.12
  256.1 0.9 copy-start.14
  257.0 5.0 copy-start.4
  257.0 5.0 copy-start.6
  268.3 5.6 copy-start.9
  273.9 3.6 copy-start.16
  282.8 5.6 copy-start.20
  282.8 5.6 copy-start.22
  295.7 27.3 %all-to-all-start.1 = ((bf16[64,32,128]{2,1,0:T(8,128)(2,1)}), bf16[64,32,128]{2,1,0:T(8,128)(2,1)}, u32[]{:S(2)}, u32[]{:S(2)}) async-start(bf16[64,32,128]{2,1,0:T(8,128)(2,1)} %copy.54), calls=%async_computation.1 | async-start | bytes 1048576 | tf_op jit(solution)/shard_map/all_to_all | solution.py:133
  305.2 76.8 %all-reduce.2.cloned.1.call-start = ((), (), s32[]{:S(2)}) async-start(), calls=%async_computation.4 | async-start | bytes 1048576 | tf_op jit(solution)/shard_map/psum | solution.py:163
  322.9 477.8 %all-gather.4.cloned.1.call-start = ((), (), s32[]{:S(2)}) async-start(), calls=%async_computation.5 | async-start | bytes 6316032 | tf_op jit(solution)/shard_map/all_gather | solution.py:162
  379.5 6.6 collective-permute-start.1
  388.2 2.5 copy-start.25
  388.2 2.5 copy-start.27
  388.2 2.5 copy-start.29
  388.2 2.5 copy-start.31
  388.2 2.5 copy-start.33
  388.2 2.5 copy-start.35
  388.2 2.5 copy-start.37
  403.3 401.3 %copy-start.1 = (f32[32,8192]{1,0:T(8,128)S(1)}, f32[32,8192]{1,0:T(8,128)}, u32[]{:S(2)}) copy-start(f32[32,8192]{1,0:T(8,128)} %param.6) | copy-start | bytes 3145732
Sparse Core Ops, SparseCore 0:
  323.1 54.8 all-reduce.1
Sparse Core Ops, SparseCore 1:
  376.6 424.1 all-gather.3
